TPU v7x, 32 devices: a whole 2x2x4 slice. The times are simulated.
32 devices in a mesh: blk: 8 (over z, core), grp: 4 (over y, x).
Axes of the slice: x: 2, y: 2, z: 4, core: 2. Of those that a mesh axis runs over, the one named last changes fastest.
Arguments:
- three_index: bfloat16 [23040, 2048], P('grp', 'blk'), may hold values from -0.359375 to 0.359375
- occ_energy: float32 [32], P('blk'), may hold values from -2 to -0.3
- vir_energy: float32 [64], replicated, may hold values from 0.2 to 3
- aux_count: int32 [4], replicated, may hold values from 1 to 5760, 22528 in all
- occ_count: int32 [8], replicated, may hold values from 1 to 4, 16 in all
Outputs:
- gamma: bfloat16 [23040, 2048], P('grp', 'blk')
Inputs may be any that keep to these rules, and one draw needn't show every extreme that they name: `aux_count`: the 4 counts sum to 22528; the largest is exactly 5760. `occ_count`: the 8 counts sum to 16; the largest is exactly 4.
All inputs are finite; a program needn't handle non-finite values.
Results may differ from a plain program's by a relative error of at most 0.018.
Values may be sent and summed in bfloat16 or wider, within the bound.
A program may use at most 64 MiB of HBM per device.

v0:
```python
import jax
import jax.numpy as jnp
from jax import lax
from jax.sharding import PartitionSpec as P

contract_first = (((0,), (0,)), ((), ()))
contract_last = (((1,), (1,)), ((), ()))


def from_behind(value, axis, steps):
    count = lax.axis_size(axis)
    pairs = [(source, (source + steps) % count) for source in range(count)]
    return lax.ppermute(value, axis, pairs)


def slab_columns(slab_energy, slab_total, vir_energy):
    columns = slab_energy.shape[0] * vir_energy.shape[0]
    col_gap = (slab_energy[:, None] - vir_energy[None, :]).reshape(columns)
    col_live = jnp.repeat(jnp.arange(slab_energy.shape[0]) < slab_total, vir_energy.shape[0])
    return (col_gap, col_live)


def divide_block(pair_block, gap_rows, gap_cols, live_rows, live_cols):
    quotient = pair_block / (gap_rows[:, None] + gap_cols[None, :])
    return jnp.where(live_rows[:, None] & live_cols[None, :], quotient, 0.0).astype(jnp.bfloat16)


def amplitudes(resident, visitor, gap_rows, gap_cols, live_rows, live_cols):
    partial_pair = lax.dot_general(
        resident, visitor, contract_first, preferred_element_type=jnp.float32
    )
    summed = lax.psum(partial_pair.astype(jnp.bfloat16), "grp").astype(jnp.float32)
    return divide_block(summed, gap_rows, gap_cols, live_rows, live_cols)


def per_device(three_index, occ_energy, vir_energy, aux_count, occ_count):
    slot_count = three_index.shape[0]
    cycle_size = lax.axis_size("blk")
    position = lax.axis_index("blk")
    aux_live = jnp.arange(slot_count) < aux_count[lax.axis_index("grp")]
    resident = jnp.where(aux_live[:, None], three_index, jnp.zeros((), jnp.bfloat16))
    gap_home, live_home = slab_columns(occ_energy, occ_count[position], vir_energy)
    amplitude = amplitudes(resident, resident, gap_home, gap_home, live_home, live_home)
    accumulated = lax.dot_general(
        resident, amplitude, contract_last, preferred_element_type=jnp.float32
    )
    slab_block, slab_energy = (resident, occ_energy)
    for offset in (1, 2):
        slab_block, slab_energy = (
            from_behind(slab_block, "blk", -1),
            from_behind(slab_energy.astype(jnp.bfloat16), "blk", -1).astype(slab_energy.dtype),
        )
        col_gap, col_live = slab_columns(
            slab_energy, occ_count[(position + offset) % cycle_size], vir_energy
        )
        amplitude = amplitudes(resident, slab_block, gap_home, col_gap, live_home, col_live)
        accumulated = accumulated + lax.dot_general(
            slab_block, amplitude, contract_last, preferred_element_type=jnp.float32
        )
        returned = jnp.dot(resident, amplitude, preferred_element_type=jnp.float32).astype(
            jnp.bfloat16
        )
        arrived = from_behind(returned, "blk", offset)
        accumulated = accumulated + arrived.astype(jnp.float32)
    return accumulated.astype(jnp.bfloat16)


def solution(mesh):
    in_specs = (P("grp", "blk"), P("blk"), P(), P(), P())
    out_specs = P("grp", "blk")
    return jax.shard_map(
        per_device, mesh=mesh, in_specs=in_specs, out_specs=out_specs, check_vma=False
    )
```

profile of v0, /device:TPU:1, one launch (start us, length us, event | category | flops | bytes accessed | tf_op | source)
XLA Modules:
  0.0 250.7 jit_solution(4971976052935671133)
XLA Ops:
  6.5 1.2 dynamic_slice.12
  7.8 0.7 iota_compare_fusion
  8.5 4.3 %broadcast_select_fusion = bf16[5760,256]{1,0:T(8,128)(2,1)S(1)} fusion(bf16[5760,256]{1,0:T(8,128)(2,1)} %param.5, pred[5760]{0:T(1024)(128)(4,1)S(1)} %iota_compare_fusion), kind=kLoop, calls=%fused_computation.7 | loop fusion | flops 1474560 | bytes 5904000 | tf_op jit(solution)/shard_map/jit(_where)/select_n | solution.py:41
  12.8 0.1 collective-permute-start
  12.9 35.6 %collective-permute-done = bf16[5760,256]{1,0:T(8,128)(2,1)} collective-permute-done((bf16[5760,256]{1,0:T(8,128)(2,1)S(1)}, bf16[5760,256]{1,0:T(8,128)(2,1)}, u32[]{:S(2)}, u32[]{:S(2)}) %collective-permute-start) | collective-permute-done | bytes 2949152 | tf_op jit(solution)/shard_map/ppermute | solution.py:13
  48.5 1.6 collective-permute-start.3
  50.1 3.8 %collective-permute-start.1 = (bf16[4]{0:T(256)(128)(2,1)S(1)}, bf16[4]{0:T(256)(128)(2,1)S(1)}, u32[]{:S(2)}, u32[]{:S(2)}) collective-permute-start(bf16[4]{0:T(256)(128)(2,1)S(1)} %convert_element_type.57), channel_id=1, source_target_pairs={{0,28},{4,0},{8,4},{12,8},{16,12},{20,16},{24,20},{28,24},{1,29},{... | collective-permute-start | bytes 32 | tf_op jit(solution)/shard_map/ppermute | solution.py:13
  53.9 0.6 fusion.10
  54.5 1.6 convolution_convert_fusion.4
  56.1 3.5 %convolution_convert_fusion.3 = bf16[256,256]{1,0:T(8,128)(2,1)} fusion(bf16[5760,256]{1,0:T(8,128)(2,1)S(1)} %broadcast_select_fusion, bf16[5760,256]{1,0:T(8,128)(2,1)} %collective-permute-done), kind=kOutput, calls=%fused_computation.9 | convolution fusion | flops 755040256 | bytes 6029312 | tf_op jit(solution)/shard_map/dot_general | solution.py:29
  59.6 23.8 %collective-permute-done.3 = bf16[5760,256]{1,0:T(8,128)(2,1)} collective-permute-done((bf16[5760,256]{1,0:T(8,128)(2,1)}, bf16[5760,256]{1,0:T(8,128)(2,1)}, u32[]{:S(2)}, u32[]{:S(2)}) %collective-permute-start.3) | collective-permute-done | bytes 2949152 | tf_op jit(solution)/shard_map/ppermute | solution.py:13
  83.4 3.5 %convolution_convert_fusion.2 = bf16[256,256]{1,0:T(8,128)(2,1)} fusion(bf16[5760,256]{1,0:T(8,128)(2,1)S(1)} %broadcast_select_fusion, bf16[5760,256]{1,0:T(8,128)(2,1)} %collective-permute-done.3), kind=kOutput, calls=%fused_computation.8 | convolution fusion | flops 755040256 | bytes 6029312 | tf_op jit(solution)/shard_map/dot_general | solution.py:29
  86.9 0.6 iota_compare_fusion.3
  87.6 0.1 and.52
  87.7 0.6 iota_compare_fusion.2
  88.4 0.1 and.57
  88.5 3.5 %collective-permute-start.4 = (bf16[4]{0:T(256)(128)(2,1)S(1)}, bf16[4]{0:T(256)(128)(2,1)S(1)}, u32[]{:S(2)}, u32[]{:S(2)}) collective-permute-start(bf16[4]{0:T(256)(128)(2,1)S(1)} %collective-permute-done.1), channel_id=1, source_target_pairs={{0,28},{4,0},{8,4},{12,8},{16,12},{20,16},{24,20},{28,24},{1,29},{... | collective-permute-start | bytes 32 | tf_op jit(solution)/shard_map/ppermute | solution.py:13
  92.0 0.8 collective-permute-done.4
  92.9 0.1 sub.63
  93.0 0.1 sub.66
  93.1 42.8 %all-reduce.3.cloned.1.call-done = (bf16[256,256]{1,0:T(8,128)(2,1)}, bf16[256,256]{1,0:T(8,128)(2,1)}, bf16[256,256]{1,0:T(8,128)(2,1)}) async-done(((bf16[256,256]{1,0:T(8,128)(2,1)}, bf16[256,256]{1,0:T(8,128)(2,1)}, bf16[256,256]{1,0:T(8,128)(2,1)}), (bf16[256,256]{1,0:T(8,128)(2,1)}, bf16[256,256]{1,0:T(8,128)(2,1)}, bf16[256,256]{1,0:T(8,128)(2,1)})) %all-reduce.3.cloned.1.call-update) | async-done | bytes 393232 | tf_op jit(solution)/shard_map/psum | solution.py:32
  135.8 3.6 %convolution_convert_fusion.1 = bf16[5760,256]{1,0:T(8,128)(2,1)} fusion(bf16[5760,256]{1,0:T(8,128)(2,1)S(1)} %broadcast_select_fusion, bf16[256,256]{1,0:T(8,128)(2,1)} %get-tuple-element.6, f32[256]{0:T(256)S(1)} %sub.66, f32[256]{0:T(256)S(1)} %sub.63, pred[256]{0:T(512)(128)(4,1)S(1)} %and.57, pred[256]{0:T(512)(128)(4,1)S(1)} %and.52), kind=kOutput, calls=%fused_computation.6 | convolution fusion | flops 756842496 | bytes 6031872 | tf_op jit(solution)/shard_map/dot_general | solution.py:60
  139.4 1.9 collective-permute-start.2
  141.3 0.6 iota_compare_fusion.1
  142.0 0.1 and.61
  142.2 1.0 convolution_convert_fusion
  143.2 1.3 collective-permute-start.5
  144.5 1.0 fusion.3
  145.5 57.4 %collective-permute-done.2 = bf16[5760,256]{1,0:T(8,128)(2,1)} collective-permute-done((bf16[5760,256]{1,0:T(8,128)(2,1)}, bf16[5760,256]{1,0:T(8,128)(2,1)}, u32[]{:S(2)}, u32[]{:S(2)}) %collective-permute-start.2) | collective-permute-done | bytes 2949152 | tf_op jit(solution)/shard_map/ppermute | solution.py:13
  202.9 3.9 %fusion.1 = f32[5760,256]{1,0:T(8,128)S(1)} fusion(f32[5760,256]{1,0:T(8,128)S(1)} %fusion.3, bf16[5760,256]{1,0:T(8,128)(2,1)} %collective-permute-done, bf16[5760,256]{1,0:T(8,128)(2,1)} %collective-permute-done.2, bf16[256,256]{1,0:T(8,128)(2,1)S(1)} %copy-done.1, f32[256]{0:T(256)S(1)} %sub.66, f32[256]{0:T(256)S(1)} %sub.63, ...), kind=kOutput, calls=%fused_computation.3 | convolution fusion | flops 759791616 | bytes 17828352 | tf_op jit(solution)/shard_map/dot_general | solution.py:57
  206.8 32.5 %collective-permute-done.5 = bf16[5760,256]{1,0:T(8,128)(2,1)S(1)} collective-permute-done((bf16[5760,256]{1,0:T(8,128)(2,1)S(1)}, bf16[5760,256]{1,0:T(8,128)(2,1)S(1)}, u32[]{:S(2)}, u32[]{:S(2)}) %collective-permute-start.5) | collective-permute-done | bytes 2949152 | tf_op jit(solution)/shard_map/ppermute | solution.py:13
  239.3 4.6 %fusion.2 = bf16[5760,256]{1,0:T(8,128)(2,1)} fusion(f32[5760,256]{1,0:T(8,128)S(1)} %fusion.1, bf16[5760,256]{1,0:T(8,128)(2,1)} %collective-permute-done.3, bf16[5760,256]{1,0:T(8,128)(2,1)S(1)} %collective-permute-done.5, bf16[256,256]{1,0:T(8,128)(2,1)S(1)} %copy-done, f32[256]{0:T(256)S(1)} %sub.69, f32[256]{0:T(256)S(1)} %sub.63, ...), kind=kOutput, calls=%fused_computation.4 | convolution fusion | flops 761266176 | bytes 14879232 | tf_op jit(solution)/shard_map/dot_general | solution.py:57
  (23 shorter events, 0.4 us)
Async XLA Ops:
  6.5 129.3 %all-reduce.3.cloned.1.call-start = ((), (), s32[]{:S(2)}) async-start(), calls=%async_computation | async-start | bytes 786432 | tf_op jit(solution)/shard_map/psum | solution.py:32
  8.4 41.6 %copy-start.4 = (f32[4]{0:T(128)S(1)}, f32[4]{0:T(128)}, u32[]{:S(2)}) copy-start(f32[4]{0:T(128)} %param.6) | copy-start | bytes 52
  8.4 45.4 %copy-start.3 = (s32[8]{0:T(128)S(1)}, s32[8]{0:T(128)}, u32[]{:S(2)}) copy-start(s32[8]{0:T(128)} %param.9) | copy-start | bytes 100
  12.8 35.7 %collective-permute-start = (bf16[5760,256]{1,0:T(8,128)(2,1)S(1)}, bf16[5760,256]{1,0:T(8,128)(2,1)}, u32[]{:S(2)}, u32[]{:S(2)}) collective-permute-start(bf16[5760,256]{1,0:T(8,128)(2,1)S(1)} %broadcast_select_fusion), channel_id=1, source_target_pairs={{0,28},{4,0},{8,4},{12,8},{16,12},{20,16},{24,20},{28,24},{1,29},{... | collective-permute-start | bytes 8847368 | tf_op jit(solution)/shard_map/ppermute | solution.py:13
  48.5 34.9 %collective-permute-start.3 = (bf16[5760,256]{1,0:T(8,128)(2,1)}, bf16[5760,256]{1,0:T(8,128)(2,1)}, u32[]{:S(2)}, u32[]{:S(2)}) collective-permute-start(bf16[5760,256]{1,0:T(8,128)(2,1)} %collective-permute-done), channel_id=1, source_target_pairs={{0,28},{4,0},{8,4},{12,8},{16,12},{20,16},{24,20},{28,24},{1,29},{... | collective-permute-start | bytes 8847368 | tf_op jit(solution)/shard_map/ppermute | solution.py:13
  50.1 38.4 %collective-permute-start.1 = (bf16[4]{0:T(256)(128)(2,1)S(1)}, bf16[4]{0:T(256)(128)(2,1)S(1)}, u32[]{:S(2)}, u32[]{:S(2)}) collective-permute-start(bf16[4]{0:T(256)(128)(2,1)S(1)} %convert_element_type.57), channel_id=1, source_target_pairs={{0,28},{4,0},{8,4},{12,8},{16,12},{20,16},{24,20},{28,24},{1,29},{... | collective-permute-start | bytes 32 | tf_op jit(solution)/shard_map/ppermute | solution.py:13
  59.6 33.2 %copy-start.5 = (f32[64]{0:T(128)S(1)}, f32[64]{0:T(128)}, u32[]{:S(2)}) copy-start(f32[64]{0:T(128)} %param.7) | copy-start | bytes 772
  88.5 4.3 %collective-permute-start.4 = (bf16[4]{0:T(256)(128)(2,1)S(1)}, bf16[4]{0:T(256)(128)(2,1)S(1)}, u32[]{:S(2)}, u32[]{:S(2)}) collective-permute-start(bf16[4]{0:T(256)(128)(2,1)S(1)} %collective-permute-done.1), channel_id=1, source_target_pairs={{0,28},{4,0},{8,4},{12,8},{16,12},{20,16},{24,20},{28,24},{1,29},{... | collective-permute-start | bytes 32 | tf_op jit(solution)/shard_map/ppermute | solution.py:13
  135.8 6.4 %copy-start = (bf16[256,256]{1,0:T(8,128)(2,1)S(1)}, bf16[256,256]{1,0:T(8,128)(2,1)}, u32[]{:S(2)}) copy-start(bf16[256,256]{1,0:T(8,128)(2,1)} %get-tuple-element.7) | copy-start | bytes 393220
  139.4 63.6 %collective-permute-start.2 = (bf16[5760,256]{1,0:T(8,128)(2,1)}, bf16[5760,256]{1,0:T(8,128)(2,1)}, u32[]{:S(2)}, u32[]{:S(2)}) collective-permute-start(bf16[5760,256]{1,0:T(8,128)(2,1)} %convolution_convert_fusion.1), channel_id=1, source_target_pairs={{0,4},{4,8},{8,12},{12,16},{16,20},{20,24},{24,28},{28,0},{1,5},{5... | collective-permute-start | bytes 8847368 | tf_op jit(solution)/shard_map/ppermute | solution.py:13
  142.2 2.3 copy-start.2
  143.2 96.1 %collective-permute-start.5 = (bf16[5760,256]{1,0:T(8,128)(2,1)S(1)}, bf16[5760,256]{1,0:T(8,128)(2,1)S(1)}, u32[]{:S(2)}, u32[]{:S(2)}) collective-permute-start(bf16[5760,256]{1,0:T(8,128)(2,1)S(1)} %convolution_convert_fusion), channel_id=1, source_target_pairs={{0,8},{4,12},{8,16},{12,20},{16,24},{20,28},{24,0},{28,4},{1,9},{5... | collective-permute-start | bytes 8847368 | tf_op jit(solution)/shard_map/ppermute | solution.py:13
  144.5 58.4 %copy-start.1 = (bf16[256,256]{1,0:T(8,128)(2,1)S(1)}, bf16[256,256]{1,0:T(8,128)(2,1)}, u32[]{:S(2)}) copy-start(bf16[256,256]{1,0:T(8,128)(2,1)} %get-tuple-element.6) | copy-start | bytes 393220
Sparse Core Ops, SparseCore 0:
  87.0 48.7 all-reduce.2
where the time goes:
time: 251 us
  waiting for transfers between devices  193 us (77%)
  matrix products  22.7 us (9%)
  between operations  13.5 us (5%)
  starting transfers between devices  12.2 us (5%)
  other arithmetic  6.95 us (3%)
  local copies, waits for them, and re-layouts  2.6 us (1%)
    ppermute x6, waiting for transfers between devices, from_behind(): return lax.ppermute(value, axis, pairs)  150 us
    psum x1, waiting for transfers between devices, amplitudes(): lax.psum(partial_pair.astype(jnp.bfloat16), 'grp').astype(jnp.float32)  42.8 us
    ppermute x6, starting transfers between devices, from_behind(): return lax.ppermute(value, axis, pairs)  12.2 us
    dot_general x3, matrix products, amplitudes(): lax.dot_general(resident, visitor, contract_first, preferred_element_type...  8.61 us
    dot_general x2, matrix products, per_device(): lax.dot_general(slab_block, amplitude, contract_last, preferred_element_t...  8.45 us
  transfers between devices with their start and end apart: 7, of which 6 were waited for; matrix products, arithmetic and copies ran while one was open for 7% of the time, Pallas kernels for 0%

commit v1 on v0

v1 whole, which is shorter than its diff:
```python
import functools

import jax
import jax.numpy as jnp
from jax import lax
from jax.experimental import pallas as pl
from jax.experimental.pallas import tpu as pltpu
from jax.sharding import PartitionSpec as P

UNIT = 128
last_last = (((1,), (1,)), ((), ()))


def dot(a, b):
    return jnp.dot(a, b, preferred_element_type=jnp.float32)


def dot_t(a, b):
    return lax.dot_general(a, b, last_last, preferred_element_type=jnp.float32)


def chunk_rows(rows):
    return max(c for c in range(16, 641, 16) if rows % c == 0)


def kernel(dims, occ_ref, aux_ref, b_ref, raw_ref, out_ref,
           sib, sib_raw, p_own, p_sib, pt_own, pt_sib, pk, bt, gap_row, gap_col,
           nb, nb_gap, vacc, acc, gsib,
           vt_o, rx_o, t_o, vt_u, rx_u, t_u,
           x_sem, m_sem, g_sem, ro_sem, ru_sem, f_sem):
    n_chip, n_grp, U, R, CH, S, D, C, nv = dims
    W = U * UNIT
    Wo = D * S
    NCH = R // CH
    blk = lax.axis_index("blk")
    grp = lax.axis_index("grp")
    chip = blk // 2
    core = blk % 2
    me = grp * 2 + core
    ahead = lax.rem(chip + 1, n_chip)
    behind = lax.rem(chip + n_chip - 1, n_chip)

    def peer(d):
        q = lax.rem(me + d, D)
        return q, {"blk": chip * 2 + q % 2, "grp": q // 2}

    sib_id = {"blk": chip * 2 + 1 - core, "grp": grp}
    ahead_id = {"blk": ahead * 2 + core, "grp": grp}
    behind_id = {"blk": behind * 2 + core, "grp": grp}

    def remote(src, dst, sems, device):
        return pltpu.make_async_remote_copy(
            src_ref=src, dst_ref=dst, send_sem=sems.at[0], recv_sem=sems.at[1],
            device_id=device, device_id_type=pl.DeviceIdType.MESH)

    barrier = pltpu.get_barrier_semaphore()
    for d in range(1, D):
        pl.semaphore_signal(barrier, inc=1, device_id=peer(d)[1], device_id_type=pl.DeviceIdType.MESH)
    for device in (ahead_id, behind_id):
        pl.semaphore_signal(barrier, inc=1, device_id=device, device_id_type=pl.DeviceIdType.MESH)
    pl.semaphore_wait(barrier, D + 1)

    other_half = pl.multiple_of((1 - core) * R, 16)
    my_half = pl.multiple_of(core * R, 16)
    swap = remote(b_ref.at[pl.ds(other_half, R), :], sib, x_sem.at[0], sib_id)
    swap_raw = remote(raw_ref, sib_raw, x_sem.at[1], sib_id)
    swap.start()
    swap_raw.start()

    first = occ_ref[chip * 2] * nv
    total = first + occ_ref[chip * 2 + 1] * nv
    ahead_first = occ_ref[ahead * 2] * nv
    ahead_total = ahead_first + occ_ref[ahead * 2 + 1] * nv
    behind_first = occ_ref[behind * 2] * nv
    behind_total = behind_first + occ_ref[behind * 2 + 1] * nv
    own_base, sib_base = core * first, (1 - core) * first
    own_count = core * (total - first) + (1 - core) * first
    sib_count = total - own_count

    def one_hot(shape, col_dim, base, count):
        i = lax.broadcasted_iota(jnp.int32, shape, col_dim)
        j = lax.broadcasted_iota(jnp.int32, shape, 1 - col_dim)
        return jnp.where((i + base == j) & (i < count), 1.0, 0.0)

    p_own[...] = one_hot((C, W), 0, own_base, own_count).astype(jnp.bfloat16)
    p_sib[...] = one_hot((C, W), 0, sib_base, sib_count).astype(jnp.bfloat16)
    pt_own[...] = one_hot((Wo, C), 1, own_base, own_count).astype(jnp.bfloat16)
    pt_sib[...] = one_hot((Wo, C), 1, sib_base, sib_count).astype(jnp.bfloat16)

    swap_raw.wait()
    exact = functools.partial(jnp.dot, precision=lax.Precision.HIGHEST, preferred_element_type=jnp.float32)
    gap_row[...] = (exact(raw_ref[...], one_hot((C, W), 0, own_base, own_count))
                    + exact(sib_raw[...], one_hot((C, W), 0, sib_base, sib_count)))
    column = jnp.sum(one_hot((Wo, C), 1, own_base, own_count) * raw_ref[0:1, :]
                     + one_hot((Wo, C), 1, sib_base, sib_count) * sib_raw[0:1, :], axis=1, keepdims=True)
    column = jnp.broadcast_to(column, (Wo, UNIT))
    for q in range(D):
        gap_col[q] = column[q * S:(q + 1) * S]
    gap_copies = [remote(gap_row, nb_gap.at[0], g_sem.at[0], ahead_id),
                  remote(gap_row, nb_gap.at[1], g_sem.at[1], behind_id)]
    for copy in gap_copies:
        copy.start()

    aux = aux_ref[grp]
    swap.wait()

    def unit_copies(j):
        return [remote(pk.at[j], nb.at[0, j], m_sem.at[0, j], ahead_id),
                remote(pk.at[j], nb.at[1, j], m_sem.at[1, j], behind_id)]

    def at_chunk(i):
        return pl.ds(pl.multiple_of(i * CH, 16), CH)

    def own_chunk(i):
        return b_ref[pl.ds(pl.multiple_of(core * R + i * CH, 16), CH), :]

    for j in range(U):
        cols = slice(j * UNIT, (j + 1) * UNIT)

        @pl.loop(0, NCH)
        def _(i):
            packed = dot(own_chunk(i), p_own[:, cols]) + dot(sib[at_chunk(i), :], p_sib[:, cols])
            row = lax.broadcasted_iota(jnp.int32, (CH, UNIT), 0) + (core * R + i * CH)
            pk[j, at_chunk(i), :] = jnp.where(row < aux, packed, 0.0).astype(jnp.bfloat16)

        for copy in unit_copies(j):
            copy.start()

    @pl.loop(0, NCH)
    def _(i):
        bt[i] = (dot_t(pt_own[...], own_chunk(i)) + dot_t(pt_sib[...], sib[at_chunk(i), :])).astype(jnp.bfloat16)

    def pk_chunk(i):
        return jnp.concatenate([pk[j, at_chunk(i), :] for j in range(U)], axis=1)

    def nb_chunk(j, i):
        return jnp.concatenate([nb[0, j, at_chunk(i), :], nb[1, j, at_chunk(i), :]], axis=1)

    def pair_sums(vt, load, N):
        vacc[:, :N] = jnp.zeros((Wo, N), jnp.float32)

        @pl.loop(0, NCH)
        def _(i):
            vacc[:, :N] += dot(bt[i], load(i))

        for q in range(D):
            vt[q] = vacc[q * S:(q + 1) * S, :N].astype(jnp.bfloat16)

    def reduce(vt, rx, t, sems, N, gap_u, valid):
        parts = []
        for d in range(1, D):
            q, device = peer(d)
            parts.append(remote(vt.at[q], rx.at[d - 1], sems.at[0, d - 1], device))
        for copy in parts:
            copy.start()
        value = vt[me].astype(jnp.float32)
        for d, copy in enumerate(parts):
            copy.wait_recv()
            value = value + rx[d].astype(jnp.float32)
        w = lax.broadcasted_iota(jnp.int32, (S, N), 0) + me * S
        u = lax.broadcasted_iota(jnp.int32, (S, N), 1)
        gap_w = jnp.concatenate([gap_col[me]] * (N // UNIT), axis=1)
        quotient = value / (gap_w + gap_u)
        t[me] = jnp.where(valid(u, w) & (w < total), quotient, 0.0).astype(jnp.bfloat16)
        backs = []
        for d in range(1, D):
            backs.append(remote(t.at[me], t.at[me], sems.at[1, d - 1], peer(d)[1]))
        for copy in backs:
            copy.start()
        for copy in backs:
            copy.wait_recv()
        for copy in parts + backs:
            copy.wait_send()

    pair_sums(vt_o, pk_chunk, W)
    reduce(vt_o, rx_o, t_o, ro_sem, W, gap_row[0:1, :], lambda u, w: u < total)

    @pl.loop(0, NCH)
    def _(i):
        acc[at_chunk(i), :] = dot_t(pk_chunk(i), t_o[...].reshape(Wo, W))

    for copy in gap_copies:
        copy.wait()

    for j in range(U):
        for copy in unit_copies(j):
            copy.wait_recv()
        pair_sums(vt_u.at[j], lambda i: nb_chunk(j, i), 2 * UNIT)
        cols = slice(j * UNIT, (j + 1) * UNIT)
        gap_u = jnp.concatenate([nb_gap[0, 0:1, cols], nb_gap[1, 0:1, cols]], axis=1)

        def valid(u, w):
            shifted = u + j * UNIT
            from_behind = (shifted < behind_total) & ((shifted >= behind_first) | (w < first))
            place = shifted - UNIT
            from_ahead = (place < ahead_total) & ((place < ahead_first) | (w >= first))
            return ((u < UNIT) & from_behind) | ((u >= UNIT) & from_ahead)

        reduce(vt_u.at[j], rx_u.at[j], t_u.at[j], ru_sem.at[j], 2 * UNIT, gap_u, valid)
        if j < U - 1:
            @pl.loop(0, NCH)
            def _(i):
                acc[at_chunk(i), :] += dot_t(nb_chunk(j, i), t_u[j].reshape(Wo, 2 * UNIT))

    def back(i):
        rows = pl.ds(pl.multiple_of(core * R + i * CH, 16), CH)
        return remote(gsib.at[at_chunk(i), :], out_ref.at[rows, :], f_sem.at[i], sib_id)

    @pl.loop(0, NCH)
    def _(i):
        value = acc[at_chunk(i), :] + dot_t(nb_chunk(U - 1, i), t_u[U - 1].reshape(Wo, 2 * UNIT))
        value = value.astype(jnp.bfloat16)
        gsib[at_chunk(i), :] = dot(value, pt_sib[...]).astype(jnp.bfloat16)
        back(i).start()
        rows = pl.ds(pl.multiple_of(core * R + i * CH, 16), CH)
        out_ref[rows, :] = dot(value, pt_own[...]).astype(jnp.bfloat16)

    @pl.loop(0, NCH)
    def _(i):
        back(i).wait()

    for j in range(U):
        for copy in unit_copies(j):
            copy.wait_send()


def call(n_chip, n_grp, U, nv, ident, occ_count, aux_count, block, raw):
    rows, C = block.shape
    R = rows // 2
    CH = chunk_rows(R)
    D = 2 * n_grp
    W = U * UNIT
    S = -(-W // (D * 16)) * 16
    Wo = D * S
    N = 2 * UNIT
    dims = (n_chip, n_grp, U, R, CH, S, D, C, nv)
    bf, f32 = jnp.bfloat16, jnp.float32
    vm, dma = pltpu.VMEM, pltpu.SemaphoreType.DMA
    scratch = [
        vm((R, C), bf), vm((8, C), f32), vm((C, W), bf), vm((C, W), bf), vm((Wo, C), bf), vm((Wo, C), bf),
        vm((U, R, UNIT), bf), vm((R // CH, Wo, CH), bf), vm((8, W), f32), vm((D, S, UNIT), f32),
        vm((2, U, R, UNIT), bf), vm((2, 8, W), f32), vm((Wo, W), f32), vm((R, Wo), f32), vm((R, C), bf),
        vm((D, S, W), bf), vm((D, S, W), bf), vm((D, S, W), bf),
        vm((U, D, S, N), bf), vm((U, D, S, N), bf), vm((U, D, S, N), bf),
        dma((2, 2)), dma((2, U, 2)), dma((2, 2)), dma((2, D, 2)), dma((U, 2, D, 2)), dma((R // CH, 2)),
    ]
    smem = pl.BlockSpec(memory_space=pltpu.SMEM)
    vmem = pl.BlockSpec(memory_space=pltpu.VMEM)
    return pl.pallas_call(
        functools.partial(kernel, dims),
        out_shape=jax.ShapeDtypeStruct((rows, C), bf),
        in_specs=[smem, smem, vmem, vmem],
        out_specs=vmem,
        scratch_shapes=scratch,
        compiler_params=pltpu.CompilerParams(
            collective_id=ident, has_side_effects=True, vmem_limit_bytes=56 * 1024 * 1024),
        cost_estimate=pl.CostEstimate(flops=12 * R * W * Wo, bytes_accessed=4 * rows * C, transcendentals=0),
    )(occ_count, aux_count, block, raw)


def solution(mesh):
    n_chip, n_grp = mesh.shape["blk"] // 2, mesh.shape["grp"]

    def per_device(three_index, occ_energy, vir_energy, aux_count, occ_count):
        C, nv = three_index.shape[1], vir_energy.shape[0]
        gap = (occ_energy[:, None] - vir_energy[None, :]).reshape(1, C)
        raw = jnp.broadcast_to(gap, (8, C))
        most = jnp.max(occ_count[0::2] + occ_count[1::2]) * nv
        full = 2 * C // UNIT
        return lax.cond(
            most <= (full - 1) * UNIT,
            functools.partial(call, n_chip, n_grp, full - 1, nv, 1),
            functools.partial(call, n_chip, n_grp, full, nv, 2),
            occ_count, aux_count, three_index, raw)

    in_specs = (P("grp", "blk"), P("blk"), P(), P(), P())
    return jax.shard_map(
        per_device, mesh=mesh, in_specs=in_specs, out_specs=P("grp", "blk"), check_vma=False)
```

time: 251 us -> 131 us (0.52)
  waiting for transfers between devices: 193 us -> 0 us
  Pallas kernels: 0 us -> 125 us
  matrix products: 22.7 us -> 0 us
  between operations: 13.5 us -> 0.67 us
  starting transfers between devices: 12.2 us -> 0 us
  other arithmetic: 6.95 us -> 1.38 us
    ppermute x6 -> x0, waiting for transfers between devices: 150 us -> none  [from_behind(): return lax.ppermute(value, axis, pairs)]
    pallas_call x0 -> x1, Pallas kernels: none -> 125 us  [call(): pl.pallas_call(functools.partial(kernel, dims), out_shape=jax.ShapeDtypeS...]
    psum x1 -> x0, waiting for transfers between devices: 42.8 us -> none  [amplitudes(): lax.psum(partial_pair.astype(jnp.bfloat16), 'grp').astype(jnp.float32)]
    dot_general x8 -> x0, matrix products: 22.7 us -> none  [the longest x3 8.61 us: amplitudes(): lax.dot_general(resident, visitor, contract_first, preferred_element_type...]
    ppermute x6 -> x0, starting transfers between devices: 12.2 us -> none  [from_behind(): return lax.ppermute(value, axis, pairs)]
    select_n x1 -> x0, other arithmetic: 4.32 us -> none  [per_device(): jnp.where(aux_live[:, None], three_index, jnp.zeros((), jnp.bfloat16))]
    lt x4 -> x0, other arithmetic: 2.54 us -> none  [the longest x3 1.89 us: slab_columns(): jnp.arange(slab_energy.shape[0]) < slab_total]
  transfers between devices with their start and end apart: 7 -> 0, of which waited for: 6 -> 0; matrix products, arithmetic and copies ran while one was open for 7% -> 0% of each run, Pallas kernels for 0% -> 0%
where the time goes in v1:
time: 131 us
  Pallas kernels  125 us (95%)
  local copies, waits for them, and re-layouts  3.18 us (2%)
  other arithmetic  1.38 us (1%)
    pallas_call x1, Pallas kernels, call(): pl.pallas_call(functools.partial(kernel, dims), out_shape=jax.ShapeDtypeS...  125 us

profile of v1, /device:TPU:1, one launch (start us, length us, event | category | flops | bytes accessed | tf_op | source)
XLA Modules:
  0.0 130.6 jit_solution(1065122585220214564)
XLA Ops:
  0.0 0.7 slice.6
  0.7 0.7 slice.7
  1.5 0.6 add_reduce_fusion
  2.8 0.7 broadcast_subtract_fusion
  3.5 0.1 sub.23
  3.6 125.4 %conditional.1 = (bf16[5760,256]{1,0:T(8,128)(2,1)S(1)}) conditional(s32[]{:T(128)} %convert_element_type.3, (s32[8]{0:T(128)}, s32[4]{0:T(128)}, bf16[5760,256]{1,0:T(8,128)(2,1)}, f32[8,256]{1,0:T(8,128)S(1)}) %tuple.11, (s32[8]{0:T(128)}, s32[4]{0:T(128)}, bf16[5760,256]{1,0:T(8,128)(2,1)}, f32[8,256]{1,0:T(8,128)S(1)}) %tuple.11), branch_computations={%region_1.0_spmd, %region_2.0_spmd} | conditional | flops 9059696640 | bytes 5898248 | solution.py:270
  3.7 125.2 %branch_1_fun.1 = bf16[5760,256]{1,0:T(8,128)(2,1)S(1)} custom-call(s32[8]{0:T(128)} %get-tuple-element.28.occ_ref, s32[4]{0:T(128)} %get-tuple-element.29.aux_ref, bf16[5760,256]{1,0:T(8,128)(2,1)} %get-tuple-element.30.b_ref, f32[8,256]{1,0:T(8,128)S(1)} %get-tuple-element.31.raw_ref), custom_call_target="tpu_custom_call" | custom-call | flops 5096079360 | bytes 5898240 | tf_op jit(solution)/shard_map/cond/branch_1_fun/pallas_call | solution.py:249
  129.0 1.6 %copy.11 = bf16[5760,256]{1,0:T(8,128)(2,1)} copy(bf16[5760,256]{1,0:T(8,128)(2,1)S(1)} %get-tuple-element.32) | data formatting | bytes 5898240
  (1 shorter events, 0.0 us)
